TPU v7x, 32 devices: a whole 2x2x4 slice. The times are simulated.
32 devices in a mesh: dp: 8 (over z, x), expert: 4 (over y, core).
Axes of the slice: x: 2, y: 2, z: 4, core: 2. Of those that a mesh axis runs over, the one named last changes fastest.
Arguments:
- x_act: bfloat16 [8, 4, 256, 4096], P('dp', None, None, 'expert'), may hold values from -16 to 16
- d_out: bfloat16 [8, 4, 256, 1536], P('dp'), may hold values from -0.375 to 0.375
- error: bfloat16 [8, 4, 4096, 1536], P('dp', None, 'expert'), may hold values from -6 to 6
- q_init: bfloat16 [1536, 256], replicated, may hold values from -6 to 6
- modality: int32 [4], replicated, may hold values from 0 to 1, as said below
- membership: int32 [8], replicated, may hold values from 0 to 3, as said below
Outputs:
- q_sum: bfloat16 [8, 1536, 256], P('dp')
- error_new: bfloat16 [8, 4, 4096, 1536], P('dp', None, 'expert')
Inputs may be any that keep to these rules, and one draw needn't show every extreme that they name: Half of the experts have modality 0 and half modality 1. `membership`: each text replica group holds exactly 2 data replicas.
All inputs are finite; a program needn't handle non-finite values.
Results may differ from a plain program's by a relative error of at most 0.005.
Values may be sent and summed in bfloat16 or wider, within the bound.
A program may use at most 128 MiB of HBM per device.

v0:
```python
import jax
import jax.numpy as jnp
from jax import lax
from jax.sharding import PartitionSpec as P

GROUPS = 4


highest = lax.Precision.HIGHEST


def split_columns(values, order, rank_width, group_mask):
    count = values.shape[0]
    experts_here = order.shape[0]
    half = experts_here // 2
    taken = jnp.take(values.reshape(count, experts_here, rank_width), order, axis=1)
    image_part = taken[:, :half].reshape(count, half * rank_width)
    text_part = taken[:, half:].reshape(count, half * rank_width)
    return (image_part, group_mask[:, None, None] * text_part)


def join_columns(image_sum, text_slots, rank_of, group_mask, rank_width, replicas, group_size):
    count = image_sum.shape[0]
    half = image_sum.shape[1] // rank_width
    image_mean = (image_sum / replicas).reshape(count, half, rank_width)
    text_mean = (jnp.sum(group_mask[:, None, None] * text_slots, axis=0) / group_size).reshape(
        count, half, rank_width
    )
    joined = jnp.concatenate([image_mean, text_mean], axis=1)
    return jnp.take(joined, rank_of, axis=1).reshape(count, 2 * half * rank_width)


def on_device(x_act, d_out, error, q_init, modality, membership):
    tok_x = x_act[0]
    grads_out = d_out[0]
    residual = error[0]
    experts_here, row_count, hidden = residual.shape
    rank_width = q_init.shape[1] // experts_here
    replicas = membership.shape[0]
    groups = GROUPS
    group_size = replicas // groups
    my_group = membership[lax.axis_index("dp")]
    group_mask = (jnp.arange(groups) == my_group).astype(jnp.float32)
    order = jnp.argsort(modality, stable=True)
    rank_of = jnp.argsort(order, stable=True)
    gradient = jnp.einsum("ktd,kth->kdh", tok_x, grads_out, preferred_element_type=jnp.float32)
    merged = (gradient + residual.astype(jnp.float32)).astype(jnp.bfloat16)
    q_blocks = q_init.reshape(hidden, experts_here, rank_width)
    left_part = jnp.einsum("kdh,hkr->dkr", merged, q_blocks, preferred_element_type=jnp.float32)
    left_part = left_part.reshape(row_count, experts_here * rank_width)
    image_part, text_part = split_columns(left_part, order, rank_width, group_mask)
    image_sum, text_slots = lax.psum((image_part, text_part), "dp")
    left_mean = join_columns(
        image_sum, text_slots, rank_of, group_mask, rank_width, replicas, group_size
    )
    blocks = left_mean.reshape(row_count, experts_here, rank_width)
    local_gram = jnp.einsum("dkr,dks->krs", blocks, blocks, precision=highest)
    gram_block = lax.psum(local_gram, "expert")
    identity = jnp.eye(rank_width, dtype=jnp.float32)
    shift_term = 0.001 * jnp.trace(gram_block, axis1=1, axis2=2) / rank_width
    factor_low = jnp.linalg.cholesky(gram_block + shift_term[:, None, None] * identity)
    inverse = jax.scipy.linalg.solve_triangular(
        factor_low, jnp.broadcast_to(identity, factor_low.shape), lower=True
    )
    p_hat = jnp.einsum("dkr,ksr->dks", blocks, inverse, precision=highest).astype(jnp.bfloat16)
    part_q = jnp.einsum("kdh,dkr->hkr", merged, p_hat, preferred_element_type=jnp.float32)
    q_local = part_q.reshape(hidden, experts_here * rank_width)
    image_part, text_part = split_columns(q_local, order, rank_width, group_mask)
    image_sum, text_slots = lax.psum((image_part, text_part), ("dp", "expert"))
    q_mean = join_columns(
        image_sum, text_slots, rank_of, group_mask, rank_width, replicas, group_size
    )
    q_sum = q_mean.astype(jnp.bfloat16)
    approx = jnp.einsum(
        "dkr,hkr->kdh",
        p_hat,
        q_sum.reshape(hidden, experts_here, rank_width),
        preferred_element_type=jnp.float32,
    )
    error_new = (merged.astype(jnp.float32) - approx).astype(jnp.bfloat16)
    return (q_sum[None], error_new[None])


def solution(mesh):
    in_specs = (
        P("dp", None, None, "expert"),
        P("dp", None, None, None),
        P("dp", None, "expert", None),
        P(),
        P(),
        P(),
    )
    out_specs = (P("dp", None, None), P("dp", None, "expert", None))
    return jax.shard_map(
        on_device, mesh=mesh, in_specs=in_specs, out_specs=out_specs, check_vma=False
    )
```

profile of v0, /device:TPU:1, one launch (start us, length us, event | category | flops | bytes accessed | tf_op | source)
XLA Modules:
  0.0 414.3 jit_solution(5845400917191781209)
XLA Ops:
  7.2 1.5 sort.31
  8.8 1.2 dynamic_slice.3
  10.0 0.6 compare_convert_fusion
  10.7 2.3 copy.30
  13.0 10.1 %fusion = bf16[4,1024,1536]{2,1,0:T(8,128)(2,1)} fusion(bf16[1,4,1024,1536]{3,2,1,0:T(8,128)(2,1)} %param.12, bf16[1,4,256,1536]{3,2,1,0:T(8,128)(2,1)S(1)} %copy-done, bf16[1,4,256,1024]{3,2,1,0:T(8,128)(2,1)} %param.10), kind=kOutput, calls=%fused_computation.5 | convolution fusion | flops 3240099840 | bytes 30408704 | tf_op jit(solution)/shard_map/ktd,kth->kdh/dot_general | solution.py:46
  23.1 8.6 %convolution_bitcast_fusion.1 = f32[1024,4,64]{0,2,1:T(8,128)S(1)} fusion(bf16[4,1024,1536]{2,1,0:T(8,128)(2,1)} %fusion, bf16[1536,4,64]{0,2,1:T(8,128)(2,1)} %bitcast.56), kind=kOutput, calls=%fused_computation.17 | convolution fusion | flops 805306368 | bytes 14417920 | tf_op jit(solution)/shard_map/kdh,hkr->dkr/dot_general | solution.py:49
  31.7 0.6 gather_fusion
  32.5 0.9 fusion.22
  33.6 1.5 broadcast_multiply_fusion.1
  35.2 0.7 sort.32
  36.0 116.6 %all-reduce.10.cloned.1.call-done = (f32[4,1024,128]{2,1,0:T(8,128)}, f32[1024,128]{0,1:T(8,128)}) async-done(((f32[4,1024,128]{2,1,0:T(8,128)}, f32[1024,128]{0,1:T(8,128)}), (f32[4,1024,128]{2,1,0:T(8,128)}, f32[1024,128]{0,1:T(8,128)})) %all-reduce.10.cloned.1.call-update) | async-done | bytes 2621456 | tf_op jit(solution)/shard_map/psum | solution.py:52
  152.6 1.9 multiply_reduce_fusion.1
  154.9 0.6 gather_fusion.1
  155.5 1.9 fusion.6
  157.7 29.9 %all-reduce.6.cloned.1.call-done = f32[4,64,64]{2,1,0:T(8,128)} async-done(((f32[4,64,64]{2,1,0:T(8,128)}), f32[4,64,64]{2,1,0:T(8,128)}) %all-reduce.6.cloned.1.call-update) | async-done | bytes 65552 | tf_op jit(solution)/shard_map/psum | solution.py:58
  187.6 1.0 select_reduce_fusion.1
  188.6 1.0 multiply_add_fusion
  189.7 1.0 fusion.16
  190.7 23.5 %custom-call.8 = f32[4,64,64]{2,1,0:T(8,128)S(1)} custom-call(f32[4,64,64]{2,1,0:T(8,128)S(1)} %fusion.16), custom_call_target="Cholesky" | custom-call | tf_op jit(solution)/shard_map/jit(cholesky)/cholesky | solution.py:61
  214.4 19.7 %custom-call.9 = f32[4,1,64,64]{2,3,1,0:T(8,128)S(1)} custom-call(f32[4,1,64,64]{3,2,1,0:T(8,128)S(1)} %select_bitcast_fusion.2), custom_call_target="InvertDiagBlocksLowerTriangular" | custom-call | tf_op jit(solution)/shard_map/jit(_solve_triangular)/vmap()/triangular_solve | solution.py:62
  234.5 1.0 fusion.4
  235.5 0.8 copy-done.2
  236.3 6.8 %convolution_bitcast_fusion = f32[1536,4,64]{0,2,1:T(8,128)S(1)} fusion(bf16[1024,4,64]{0,2,1:T(8,128)(2,1)S(1)} %fusion.4, bf16[4,1024,1536]{2,1,0:T(8,128)(2,1)} %fusion), kind=kOutput, calls=%fused_computation.10 | convolution fusion | flops 805306368 | bytes 14680064 | tf_op jit(solution)/shard_map/kdh,dkr->hkr/dot_general | solution.py:66
  243.1 0.7 gather_fusion.2
  244.1 1.0 fusion.21
  245.3 2.0 broadcast_multiply_fusion
  247.3 140.4 %all-reduce.8.cloned.1.call-done = (f32[4,1536,128]{2,1,0:T(8,128)}, f32[1536,128]{0,1:T(8,128)}) async-done(((f32[4,1536,128]{2,1,0:T(8,128)}, f32[1536,128]{0,1:T(8,128)}), (f32[4,1536,128]{2,1,0:T(8,128)}, f32[1536,128]{0,1:T(8,128)})) %all-reduce.8.cloned.1.call-update) | async-done | bytes 3932176 | tf_op jit(solution)/shard_map/psum | solution.py:69
  387.7 2.3 multiply_reduce_fusion
  390.4 0.6 gather_fusion.3
  391.0 1.1 bitcast_convert_fusion
  392.1 13.4 %fusion.1 = bf16[1,4,1024,1536]{3,2,1,0:T(8,128)(2,1)} fusion(bf16[1024,4,64]{0,2,1:T(8,128)(2,1)} %copy-done.2, bf16[1536,4,64]{0,2,1:T(8,128)(2,1)} %bitcast_convert_fusion, bf16[4,1024,1536]{2,1,0:T(8,128)(2,1)} %fusion), kind=kOutput, calls=%fused_computation.7 | convolution fusion | flops 824180736 | bytes 26476544 | tf_op jit(solution)/shard_map/dkr,hkr->kdh/dot_general | solution.py:74
  405.5 2.3 copy.37
  (44 shorter events, 2.8 us)
Async XLA Ops:
  7.2 5.8 %copy-start = (bf16[1,4,256,1536]{3,2,1,0:T(8,128)(2,1)S(1)}, bf16[1,4,256,1536]{3,2,1,0:T(8,128)(2,1)}, u32[]{:S(2)}) copy-start(bf16[1,4,256,1536]{3,2,1,0:T(8,128)(2,1)} %param.11) | copy-start | bytes 9437188
  7.2 145.4 %all-reduce.10.cloned.1.call-start = ((), (), s32[]{:S(2)}) async-start(), calls=%async_computation.2 | async-start | bytes 5242880 | tf_op jit(solution)/shard_map/psum | solution.py:52
  35.2 152.4 %all-reduce.6.cloned.1.call-start = ((), (), s32[]{:S(2)}) async-start(), calls=%async_computation | async-start | bytes 262144 | tf_op jit(solution)/shard_map/psum | solution.py:58
  152.6 2.2 copy-start.4
  157.4 230.3 %all-reduce.8.cloned.1.call-start = ((), (), s32[]{:S(2)}) async-start(), calls=%async_computation.1 | async-start | bytes 7864320 | tf_op jit(solution)/shard_map/psum | solution.py:69
  235.5 0.8 copy-start.2
  387.7 2.6 copy-start.3
  392.1 15.6 %copy-start.1 = (bf16[1,4,256,1536]{3,2,1,0:T(8,128)(2,1)S(1)}, bf16[1,4,256,1536]{3,2,1,0:T(8,128)(2,1)}, u32[]{:S(2)}) copy-start(bf16[1,4,256,1536]{3,2,1,0:T(8,128)(2,1)} %param.11) | copy-start | bytes 9437188
Sparse Core Ops, SparseCore 0:
  35.3 117.2 all-reduce.9
  157.5 29.9 all-reduce.5
  247.4 140.2 all-reduce.7
where the time goes:
time: 417 us; the launch traced here: 414 us
  waiting for transfers between devices  287 us (69%)
  other arithmetic  58.9 us (14%)
  matrix products  42.2 us (10%)
  between operations  14 us (3%)
  local copies, waits for them, and re-layouts  11.9 us (3%)
    psum x1, waiting for transfers between devices, on_device(): image_sum, text_slots = lax.psum((image_part, text_part), ('dp', 'expert'))  140 us
    psum x1, waiting for transfers between devices, on_device(): image_sum, text_slots = lax.psum((image_part, text_part), 'dp')  117 us
    psum x1, waiting for transfers between devices, on_device(): gram_block = lax.psum(local_gram, 'expert')  29.9 us
    another operation x4, other arithmetic, on_device(): jnp.linalg.cholesky(gram_block + shift_term[:, None, None] * identity)  23.6 us
    another operation x3, other arithmetic, on_device(): jax.scipy.linalg.solve_triangular(factor_low, jnp.broadcast_to(identity,...  19.8 us
    dot_general x1, matrix products, on_device(): jnp.einsum('dkr,hkr->kdh', p_hat, q_sum.reshape(hidden, experts_here, ran...  13.4 us
    dot_general x1, matrix products, on_device(): jnp.einsum('ktd,kth->kdh', tok_x, grads_out, preferred_element_type=jnp.f...  10.1 us
    dot_general x1, matrix products, on_device(): jnp.einsum('kdh,hkr->dkr', merged, q_blocks, preferred_element_type=jnp.f...  8.58 us
  transfers between devices with their start and end apart: 3, of which 3 were waited for; matrix products, arithmetic and copies ran while one was open for 0% of the time, Pallas kernels for 0%

commit v1 on v0

--- a/solution.py
+++ b/solution.py
@@ -1,6 +1,10 @@
+import functools
+
 import jax
 import jax.numpy as jnp
 from jax import lax
+from jax.experimental import pallas as pl
+from jax.experimental.pallas import tpu as pltpu
 from jax.sharding import PartitionSpec as P
 
 GROUPS = 4
@@ -81,6 +85,477 @@
     return (q_sum[None], error_new[None])
 
 
+MESH = pl.DeviceIdType.MESH
+F32 = jnp.float32
+BF16 = jnp.bfloat16
+
+
+def compress_kernel(
+    n_dp, n_ex, group_size,
+    x_hbm, d_hbm, err_hbm, q_ref, modality, membership,
+    merged_hbm, pt_out, qt_out,
+    xs, ds, merged, lsend, lrecv, msend, lmean, gsend, grecv, pt_ref,
+    qpart, qr1, qs2, qr2, q3, qr3, q4, qf,
+    x_sem, d_sem, e_sem, m_sem, ls_sem, lr_sem, ms_sem, mr_sem, gs_sem, gr_sem,
+    s1_sem, r1_sem, s2_sem, r2_sem, s3_sem, r3_sem, s4_sem, r4_sem,
+    s5_sem, r5_sem,
+):
+    dp = lax.axis_index("dp")
+    ex = lax.axis_index("expert")
+    core, row = ex % 2, ex // 2
+    ex_core = row * 2 + (1 - core)
+    ex_row = (1 - row) * 2 + core
+    ex_far = (1 - row) * 2 + (1 - core)
+    experts, tokens, rows = xs.shape
+    hidden = ds.shape[2]
+    width = q_ref.shape[1]
+    rank = width // experts
+    step_rows = rows // n_dp
+    slab = hidden // n_ex
+    part = width // n_dp
+
+    def remote(src, dst, send, recv, dp_to, ex_to):
+        return pltpu.make_async_remote_copy(
+            src_ref=src, dst_ref=dst, send_sem=send, recv_sem=recv,
+            device_id=(dp_to, ex_to), device_id_type=MESH,
+        )
+
+    def rows_of(c, size):
+        return pl.ds(pl.multiple_of(c * size, size), size)
+
+    def err_copy(s):
+        at = rows_of((dp + 1 + s) % n_dp, step_rows)
+        return pltpu.make_async_copy(err_hbm.at[:, at, :], merged.at[:, at, :], e_sem.at[s])
+
+    def merged_copy(s):
+        at = rows_of((dp + 1 + s) % n_dp, step_rows)
+        return pltpu.make_async_copy(merged.at[:, at, :], merged_hbm.at[:, at, :], m_sem.at[s])
+
+    x_copies = [pltpu.make_async_copy(x_hbm.at[k], xs.at[k], x_sem.at[k]) for k in range(experts)]
+    d_copies = [pltpu.make_async_copy(d_hbm.at[k], ds.at[k], d_sem.at[k]) for k in range(experts)]
+    for k in range(experts):
+        x_copies[k].start()
+        d_copies[k].start()
+    for s in range(n_dp):
+        err_copy(s).start()
+
+    barrier = pltpu.get_barrier_semaphore()
+    for s in range(1, n_dp):
+        pl.semaphore_signal(barrier, inc=1, device_id=((dp + s) % n_dp, ex), device_id_type=MESH)
+    for other in (ex_core, ex_row, ex_far):
+        pl.semaphore_signal(barrier, inc=1, device_id=(dp, other), device_id_type=MESH)
+    pl.semaphore_wait(barrier, n_dp - 1 + 3)
+
+    for k in range(experts):
+        x_copies[k].wait()
+        d_copies[k].wait()
+
+    lane = lax.broadcasted_iota(jnp.int32, (1, width), 1)
+
+    def left_copy(c, src):
+        return remote(lsend.at[c], lrecv.at[src], ls_sem.at[c], lr_sem.at[src], c, ex)
+
+    def left_step(s, carry):
+        c = (dp + 1 + s) % n_dp
+        at = rows_of(c, step_rows)
+        err_copy(s).wait()
+        total = jnp.zeros((step_rows, width), F32)
+        for k in range(experts):
+            xk = xs[k, :, at]
+            mine = jnp.zeros((step_rows, width), F32)
+            for n in range(3):
+                cols = slice(n * (hidden // 3), (n + 1) * (hidden // 3))
+                grad = lax.dot_general(
+                    xk, ds[k, :, cols], (((0,), (0,)), ((), ())), preferred_element_type=F32
+                )
+                both = (grad + merged[k, at, cols].astype(F32)).astype(BF16)
+                merged[k, at, cols] = both
+                mine += jnp.dot(both, q_ref[cols, :], preferred_element_type=F32)
+            total += jnp.where(lane // rank == k, mine, 0.0)
+        merged_copy(s).start()
+
+        @pl.when(s < n_dp - 1)
+        def _():
+            lsend[c] = total.astype(BF16)
+            left_copy(c, dp).start()
+
+        @pl.when(s == n_dp - 1)
+        def _():
+            lrecv[dp] = total.astype(BF16)
+
+        return carry
+
+    lax.fori_loop(0, n_dp, left_step, 0)
+
+    def wait_left(s, carry):
+        left_copy((dp + s) % n_dp, (dp + n_dp - s) % n_dp).wait_recv()
+        return carry
+
+    lax.fori_loop(1, n_dp, wait_left, 0)
+
+    image = jnp.zeros((1, width), F32)
+    for k in range(experts):
+        flag = jnp.where(modality[k] == 0, 1.0, 0.0)
+        image = jnp.where(lane // rank == k, flag, image)
+
+    def mean_copy(i, src):
+        return remote(msend.at[i], lmean.at[src], ms_sem.at[i], mr_sem.at[src], i, ex)
+
+    def mean_step(s, carry):
+        i = (dp + 1 + s) % n_dp
+        acc = jnp.zeros((step_rows, width), F32)
+        for j in range(n_dp):
+            same = jnp.where(membership[i] == membership[j], 1.0 / group_size, 0.0)
+            weight = jnp.where(image > 0.5, 1.0 / n_dp, same)
+            acc += weight * lrecv[j].astype(F32)
+
+        @pl.when(s < n_dp - 1)
+        def _():
+            msend[i] = acc.astype(BF16)
+            mean_copy(i, dp).start()
+
+        @pl.when(s == n_dp - 1)
+        def _():
+            lmean[dp] = acc.astype(BF16)
+
+        return carry
+
+    lax.fori_loop(0, n_dp, mean_step, 0)
+
+    def gram_of(j):
+        block = lmean[j]
+        return lax.dot_general(block, block, (((0,), (0,)), ((), ())), preferred_element_type=F32)
+
+    def gram_step(s, acc):
+        j = (dp + n_dp - s) % n_dp
+        mean_copy((dp + s) % n_dp, j).wait_recv()
+        return acc + gram_of(j)
+
+    gram = lax.fori_loop(1, n_dp, gram_step, gram_of(dp))
+    pairs = experts // 2
+    pair_lane = lax.broadcasted_iota(jnp.int32, (rank, 2 * rank), 1)
+    pair_row = lax.broadcasted_iota(jnp.int32, (rank, 2 * rank), 0)
+    low = pair_lane < rank
+    for p in range(pairs):
+        b = 2 * p * rank
+        gsend[p] = jnp.where(
+            low, gram[b : b + rank, b : b + 2 * rank], gram[b + rank : b + 2 * rank, b : b + 2 * rank]
+        )
+    grecv[ex] = gsend[...]
+    others = (ex_core, ex_row, ex_far)
+    gram_sends = [
+        remote(gsend, grecv.at[ex], gs_sem.at[n], gr_sem.at[n], dp, other)
+        for n, other in enumerate(others)
+    ]
+    for copy in gram_sends:
+        copy.start()
+    for n, other in enumerate(others):
+        remote(gsend, grecv.at[other], gs_sem.at[n], gr_sem.at[n], dp, other).wait_recv()
+    full = grecv[0]
+    for e in range(1, n_ex):
+        full = full + grecv[e]
+
+    spots = (pair_lane == pair_row, pair_lane == pair_row + rank)
+    work = []
+    for odd in range(2):
+        diag, unit = spots[odd], spots[1 - odd]
+        trace = jnp.sum(jnp.where(diag, full, 0.0), axis=(1, 2), keepdims=True)
+        a = full + jnp.where(diag, 0.001 * trace / rank, 0.0)
+        here = low if odd == 0 else jnp.logical_not(low)
+        work.append(jnp.where(here, a, jnp.where(unit, 1.0, 0.0)))
+    done = [[], []]
+    for j in range(rank):
+        r = j % 8
+        left_rows = rank - (j - r)
+        below = lax.broadcasted_iota(jnp.int32, (1, left_rows, 1), 1) > r
+        for odd in range(2):
+            w = work[odd]
+            at = j + odd * rank
+            pivot = w[:, r : r + 1, :]
+            scaled = pivot / w[:, r : r + 1, at : at + 1]
+            work[odd] = w - jnp.where(below, w[:, :, at : at + 1], 0.0) * scaled
+        if r == 7:
+            for odd in range(2):
+                done[odd].append(work[odd][:, :8, :])
+                work[odd] = work[odd][:, 8:, :]
+    blocks = []
+    for p in range(pairs):
+        for odd in range(2):
+            w = jnp.concatenate([chunk[p] for chunk in done[odd]], axis=0)
+            pivots = jnp.sum(jnp.where(spots[odd], w, 0.0), axis=1, keepdims=True)
+            keep = jnp.logical_not(low) if odd == 0 else low
+            inverse = jnp.where(keep, w, 0.0) / jnp.sqrt(pivots)
+            inverse = pltpu.roll(inverse, rank, 1)
+            zero = jnp.zeros((rank, 2 * rank), F32)
+            blocks.append(
+                jnp.concatenate([inverse if q == p else zero for q in range(pairs)], axis=1)
+            )
+    inv = jnp.concatenate(blocks, axis=0)
+    inv_high = inv.astype(BF16)
+    inv_low = (inv - inv_high.astype(F32)).astype(BF16)
+    for j in range(n_dp):
+        block = lmean[j]
+        dims = (((1,), (1,)), ((), ()))
+        p_t = lax.dot_general(inv_high, block, dims, preferred_element_type=F32)
+        p_t += lax.dot_general(inv_low, block, dims, preferred_element_type=F32)
+        pt_ref[:, j * step_rows : (j + 1) * step_rows] = p_t.astype(BF16)
+    pt_out[...] = pt_ref[...]
+
+    def k_rows(k):
+        return pl.ds(k * rank, rank)
+
+    def core_copy(k, n):
+        slab_at = (ex_core, ex_far)[n]
+        return remote(
+            qpart.at[slab_at, k_rows(k), :], qr1.at[n, k_rows(k), :],
+            s1_sem.at[n, k], r1_sem.at[n, k], dp, ex_core,
+        )
+
+    def row_copy(k):
+        return remote(
+            qs2.at[k_rows(k), :], qr2.at[k_rows(k), :], s2_sem.at[k], r2_sem.at[k], dp, ex_row
+        )
+
+    def part_copy(c, src):
+        return remote(
+            q3.at[rows_of(c, part), :], qr3.at[src], s3_sem.at[c], r3_sem.at[src], c, ex
+        )
+
+    per = rank // part
+
+    def stage_one(k):
+        p_k = pt_ref[k * rank : (k + 1) * rank, :]
+        for e in range(n_ex):
+            out = jnp.dot(
+                p_k, merged[k, :, e * slab : (e + 1) * slab], preferred_element_type=F32
+            )
+            qpart[e, k * rank : (k + 1) * rank, :] = out.astype(BF16)
+        core_copy(k, 1).start()
+        core_copy(k, 0).start()
+
+    def stage_two(k):
+        core_copy(k, 1).wait_recv()
+        at = slice(k * rank, (k + 1) * rank)
+        qs2[at, :] = (qpart[ex_row, at, :].astype(F32) + qr1[1, at, :].astype(F32)).astype(BF16)
+        row_copy(k).start()
+
+    def stage_three(k):
+        core_copy(k, 0).wait_recv()
+        row_copy(k).wait_recv()
+        at = slice(k * rank, (k + 1) * rank)
+        q3[at, :] = (
+            qpart[ex, at, :].astype(F32) + qr1[0, at, :].astype(F32) + qr2[at, :].astype(F32)
+        ).astype(BF16)
+        for c in range(k * per, (k + 1) * per):
+
+            @pl.when(dp != c)
+            def _():
+                part_copy(c, dp).start()
+
+            @pl.when(dp == c)
+            def _():
+                qr3[c] = q3[c * part : (c + 1) * part, :]
+
+    for k in range(experts + 2):
+        if k < experts:
+            stage_one(k)
+        if 1 <= k <= experts:
+            stage_two(k - 1)
+        if k >= 2:
+            stage_three(k - 2)
+
+    def wait_part(s, carry):
+        part_copy((dp + s) % n_dp, (dp + n_dp - s) % n_dp).wait_recv()
+        return carry
+
+    lax.fori_loop(1, n_dp, wait_part, 0)
+    my_image = modality[dp // per] == 0
+
+    def back_copy(i, src):
+        return remote(
+            q4.at[i], qf.at[ex, rows_of(src, part), :], s4_sem.at[i], r4_sem.at[src], i, ex
+        )
+
+    def back_step(s, carry):
+        i = (dp + 1 + s) % n_dp
+        acc = jnp.zeros((part, slab), F32)
+        for j in range(n_dp):
+            same = jnp.where(membership[i] == membership[j], 1.0 / group_size, 0.0)
+            acc += jnp.where(my_image, 1.0 / n_dp, same) * qr3[j].astype(F32)
+
+        @pl.when(s < n_dp - 1)
+        def _():
+            q4[i] = acc.astype(BF16)
+            back_copy(i, dp).start()
+
+        @pl.when(s == n_dp - 1)
+        def _():
+            qf[ex, rows_of(dp, part), :] = acc.astype(BF16)
+
+        return carry
+
+    lax.fori_loop(0, n_dp, back_step, 0)
+
+    def spread(c, n):
+        held, to = ((ex, ex_core), (ex, ex_row), (ex_row, ex_core))[n]
+        at = rows_of(c, part)
+        return remote(
+            qf.at[held, at, :], qf.at[held, at, :], s5_sem.at[n, c], r5_sem.at[n, c], dp, to
+        )
+
+    def spread_step(s, carry):
+        c = (dp + n_dp - s) % n_dp
+
+        @pl.when(s > 0)
+        def _():
+            back_copy((dp + s) % n_dp, c).wait_recv()
+
+        spread(c, 1).start()
+        spread(c, 0).start()
+        return carry
+
+    lax.fori_loop(0, n_dp, spread_step, 0)
+
+    def forward_step(s, carry):
+        c = (dp + n_dp - s) % n_dp
+        spread(c, 1).wait_recv()
+        spread(c, 2).start()
+        return carry
+
+    lax.fori_loop(0, n_dp, forward_step, 0)
+
+    def last_step(s, carry):
+        c = (dp + n_dp - s) % n_dp
+        spread(c, 0).wait_recv()
+        spread(c, 2).wait_recv()
+        return carry
+
+    lax.fori_loop(0, n_dp, last_step, 0)
+    for e in range(n_ex):
+        qt_out[:, e * slab : (e + 1) * slab] = qf[e]
+
+    def drain(s, carry):
+        i = (dp + s) % n_dp
+        left_copy(i, dp).wait_send()
+        mean_copy(i, dp).wait_send()
+        part_copy(i, dp).wait_send()
+        back_copy(i, dp).wait_send()
+        return carry
+
+    lax.fori_loop(1, n_dp, drain, 0)
+
+    def drain_all(c, carry):
+        for n in range(3):
+            spread(c, n).wait_send()
+        merged_copy(c).wait()
+        return carry
+
+    lax.fori_loop(0, n_dp, drain_all, 0)
+    for k in range(experts):
+        core_copy(k, 0).wait_send()
+        core_copy(k, 1).wait_send()
+        row_copy(k).wait_send()
+    for copy in gram_sends:
+        copy.wait_send()
+
+
+def residual_kernel(pt_ref, qt_ref, merged_ref, out_ref):
+    approx = lax.dot_general(
+        pt_ref[...], qt_ref[...], (((0,), (0,)), ((), ())), preferred_element_type=F32
+    )
+    out_ref[0] = (merged_ref[0].astype(F32) - approx).astype(BF16)
+
+
+def tiled_form(n_dp, n_ex, x_act, d_out, error, q_init, modality, membership):
+    experts, tokens, rows = x_act.shape[1:]
+    hidden = d_out.shape[3]
+    width = q_init.shape[1]
+    rank = width // experts
+    slab, part, step_rows = hidden // n_ex, width // n_dp, rows // n_dp
+    group_size = membership.shape[0] // GROUPS
+    any_spec = pl.BlockSpec(memory_space=pl.ANY)
+    vmem = pl.BlockSpec(memory_space=pltpu.VMEM)
+    smem = pl.BlockSpec(memory_space=pltpu.SMEM)
+    dma = pltpu.SemaphoreType.DMA
+    merged, p_t, q_t = pl.pallas_call(
+        functools.partial(compress_kernel, n_dp, n_ex, group_size),
+        out_shape=(
+            jax.ShapeDtypeStruct((experts, rows, hidden), BF16),
+            jax.ShapeDtypeStruct((width, rows), BF16),
+            jax.ShapeDtypeStruct((width, hidden), BF16),
+        ),
+        in_specs=[any_spec, any_spec, any_spec, vmem, smem, smem],
+        out_specs=(any_spec, vmem, vmem),
+        scratch_shapes=[
+            pltpu.VMEM((experts, tokens, rows), BF16),
+            pltpu.VMEM((experts, tokens, hidden), BF16),
+            pltpu.VMEM((experts, rows, hidden), BF16),
+            pltpu.VMEM((n_dp, step_rows, width), BF16),
+            pltpu.VMEM((n_dp, step_rows, width), BF16),
+            pltpu.VMEM((n_dp, step_rows, width), BF16),
+            pltpu.VMEM((n_dp, step_rows, width), BF16),
+            pltpu.VMEM((experts // 2, rank, 2 * rank), F32),
+            pltpu.VMEM((n_ex, experts // 2, rank, 2 * rank), F32),
+            pltpu.VMEM((width, rows), BF16),
+            pltpu.VMEM((n_ex, width, slab), BF16),
+            pltpu.VMEM((2, width, slab), BF16),
+            pltpu.VMEM((width, slab), BF16),
+            pltpu.VMEM((width, slab), BF16),
+            pltpu.VMEM((width, slab), BF16),
+            pltpu.VMEM((n_dp, part, slab), BF16),
+            pltpu.VMEM((n_dp, part, slab), BF16),
+            pltpu.VMEM((n_ex, width, slab), BF16),
+            dma((experts,)), dma((experts,)), dma((n_dp,)), dma((n_dp,)),
+            dma((n_dp,)), dma((n_dp,)), dma((n_dp,)), dma((n_dp,)),
+            dma((3,)), dma((3,)),
+            dma((2, experts)), dma((2, experts)), dma((experts,)), dma((experts,)),
+            dma((n_dp,)), dma((n_dp,)), dma((n_dp,)), dma((n_dp,)),
+            dma((3, n_dp)), dma((3, n_dp)),
+        ],
+        compiler_params=pltpu.CompilerParams(
+            collective_id=0, has_side_effects=True, vmem_limit_bytes=50 * 2**20
+        ),
+        cost_estimate=pl.CostEstimate(
+            flops=12 * experts * rows * hidden * tokens // 4,
+            bytes_accessed=4 * experts * rows * hidden,
+            transcendentals=0,
+        ),
+        name="compress",
+    )(x_act[0], d_out[0], error[0], q_init, modality, membership)
+    block = rows // 4
+    error_new = pl.pallas_call(
+        residual_kernel,
+        grid=(experts, rows // block),
+        out_shape=jax.ShapeDtypeStruct((experts, rows, hidden), BF16),
+        in_specs=[
+            pl.BlockSpec((rank, block), lambda k, r: (k, r)),
+            pl.BlockSpec((rank, hidden), lambda k, r: (k, 0)),
+            pl.BlockSpec((1, block, hidden), lambda k, r: (k, r, 0)),
+        ],
+        out_specs=pl.BlockSpec((1, block, hidden), lambda k, r: (k, r, 0)),
+        compiler_params=pltpu.CompilerParams(vmem_limit_bytes=32 * 2**20),
+        name="residual",
+    )(p_t, q_t, merged)
+    return (q_t.T[None], error_new[None])
+
+
+def tiles(n_dp, n_ex, x_act, d_out, error, q_init, modality, membership):
+    experts, _, rows = x_act.shape[1:]
+    hidden, width = q_init.shape
+    rank = width // experts
+    return (
+        n_ex == 4
+        and experts % 2 == 0
+        and 2 * rank == 128
+        and experts % 2 == 0
+        and rank % (width // n_dp) == 0
+        and (width // n_dp) % 16 == 0
+        and (rows // n_dp) % 128 == 0
+        and (hidden // n_ex) % 128 == 0
+        and (hidden // 3) % 128 == 0
+    )
+
+
 def solution(mesh):
     in_specs = (
         P("dp", None, None, "expert"),
@@ -91,6 +566,13 @@
         P(),
     )
     out_specs = (P("dp", None, None), P("dp", None, "expert", None))
+    n_dp, n_ex = mesh.shape["dp"], mesh.shape["expert"]
+
+    def body(*args):
+        if tiles(n_dp, n_ex, *args):
+            return tiled_form(n_dp, n_ex, *args)
+        return on_device(*args)
+
     return jax.shard_map(
-        on_device, mesh=mesh, in_specs=in_specs, out_specs=out_specs, check_vma=False
-    )
+        body, mesh=mesh, in_specs=in_specs, out_specs=out_specs, check_vma=False
+    )

time: 417 us -> 95.7 us (0.23)
  waiting for transfers between devices: 287 us -> 0 us
  Pallas kernels: 0 us -> 86.6 us
  other arithmetic: 58.9 us -> 0 us
  matrix products: 42.2 us -> 0 us
  between operations: 14 us -> 0.66 us
    psum x3 -> x0, waiting for transfers between devices: 287 us -> none  [the longest x1 140 us: on_device(): image_sum, text_slots = lax.psum((image_part, text_part), ('dp', 'expert'))]
    pallas_call x0 -> x2, Pallas kernels: none -> 86.6 us  [the longest x1 76.1 us: tiled_form(): pl.pallas_call(functools.partial(compress_kernel, n_dp, n_ex, group_size)...]
    another operation x7 -> x0, other arithmetic: 43.4 us -> none  [the longest x4 23.6 us: on_device(): jnp.linalg.cholesky(gram_block + shift_term[:, None, None] * identity)]
    dot_general x6 -> x0, matrix products: 41.8 us -> none  [the longest x1 13.4 us: on_device(): jnp.einsum('dkr,hkr->kdh', p_hat, q_sum.reshape(hidden, experts_here, ran...]
    reduce_sum x3 -> x0, other arithmetic: 5.25 us -> none  [the longest x2 4.22 us: join_columns(): jnp.sum(group_mask[:, None, None] * text_slots, axis=0) / group_size]
  transfers between devices with their start and end apart: 3 -> 0, of which waited for: 3 -> 0; matrix products, arithmetic and copies ran while one was open for 0% -> 0% of each run, Pallas kernels for 0% -> 0%
where the time goes in v1:
time: 95.7 us; the launch traced here: 95.5 us
  Pallas kernels  86.6 us (90%)
  local copies, waits for them, and re-layouts  8.16 us (9%)
    pallas_call x1, Pallas kernels, tiled_form(): pl.pallas_call(functools.partial(compress_kernel, n_dp, n_ex, group_size)...  76.1 us
    pallas_call x1, Pallas kernels, tiled_form(): pl.pallas_call(residual_kernel, grid=(experts, rows // block), out_shape=...  10.6 us
    unnamed x9, local copies, waits for them, and re-layouts  8.16 us

profile of v1, /device:TPU:1, one launch (start us, length us, event | category | flops | bytes accessed | tf_op | source)
XLA Modules:
  0.0 95.5 jit_solution(274051346836775344)
XLA Ops:
  0.6 0.0 copy-start.1
  0.6 1.1 %copy-done.1 = bf16[1536,256]{1,0:T(8,128)(2,1)S(1)} copy-done((bf16[1536,256]{1,0:T(8,128)(2,1)S(1)}, bf16[1536,256]{1,0:T(8,128)(2,1)}, u32[]{:S(2)}) %copy-start.1) | copy-done | bytes 786456
  1.8 0.0 copy-start.2
  1.8 0.7 copy-done.2
  2.4 0.0 copy-start.3
  2.4 0.7 copy-done.3
  3.1 76.1 %compress.1 = (bf16[4,1024,1536]{2,1,0:T(8,128)(2,1)}, bf16[256,1024]{1,0:T(8,128)(2,1)S(1)}, bf16[256,1536]{1,0:T(8,128)(2,1)S(1)}) custom-call(bf16[4,256,1024]{2,1,0:T(8,128)(2,1)} %bitcast.11, bf16[4,256,1536]{2,1,0:T(8,128)(2,1)} %bitcast.10, bf16[4,1024,1536]{2,1,0:T(8,128)(2,1)} %bitcast.8, bf16[1536,256]{1,0:T(8,128)(2,1)S(1)} %copy-done.1, ...), custom_call_target="tpu_custom_call" | custom-call | flops 4831838208 | bytes 25165824 | tf_op jit(solution)/shard_map/compress/pallas_call | solution.py:480
  79.1 0.0 copy-start
  79.1 4.6 %copy-done = bf16[4,1024,1536]{2,1,0:T(8,128)(2,1)S(1)} copy-done((bf16[4,1024,1536]{2,1,0:T(8,128)(2,1)S(1)}, bf16[4,1024,1536]{2,1,0:T(8,128)(2,1)}, u32[]{:S(2)}) %copy-start) | copy-done | bytes 12582936
  83.7 10.6 %residual.1 = bf16[4,1024,1536]{2,1,0:T(8,128)(2,1)} custom-call(bf16[256,1024]{1,0:T(8,128)(2,1)S(1)} %get-tuple-element.6.pt_ref, bf16[256,1536]{1,0:T(8,128)(2,1)S(1)} %get-tuple-element.5.qt_ref, bf16[4,1024,1536]{2,1,0:T(8,128)(2,1)S(1)} %copy-done), custom_call_target="tpu_custom_call" | custom-call | tf_op jit(solution)/shard_map/residual/pallas_call | solution.py:526
  94.3 1.2 %copy.8 = bf16[1,1536,256]{2,1,0:T(8,128)(2,1)} copy(bf16[1,1536,256]{1,2,0:T(8,128)(2,1)S(1)} %bitcast.7) | data formatting | bytes 1572864
Async XLA Ops:
  0.6 1.1 %copy-start.1 = (bf16[1536,256]{1,0:T(8,128)(2,1)S(1)}, bf16[1536,256]{1,0:T(8,128)(2,1)}, u32[]{:S(2)}) copy-start(bf16[1536,256]{1,0:T(8,128)(2,1)} %q_ref.1) | copy-start | bytes 2359300
  1.8 0.7 copy-start.2
  2.4 0.7 copy-start.3
  79.1 4.6 %copy-start = (bf16[4,1024,1536]{2,1,0:T(8,128)(2,1)S(1)}, bf16[4,1024,1536]{2,1,0:T(8,128)(2,1)}, u32[]{:S(2)}) copy-start(bf16[4,1024,1536]{2,1,0:T(8,128)(2,1)} %get-tuple-element.7.merged_ref) | copy-start | bytes 37748740

commit v2 on v1

--- a/solution.py
+++ b/solution.py
@@ -92,11 +92,11 @@
 
 def compress_kernel(
     n_dp, n_ex, group_size,
-    x_hbm, d_hbm, err_hbm, q_ref, modality, membership,
-    merged_hbm, pt_out, qt_out,
-    xs, ds, merged, lsend, lrecv, msend, lmean, gsend, grecv, pt_ref,
+    x_hbm, d_hbm, err_hbm, q_hbm, modality_hbm, membership_hbm,
+    merged_hbm, pt_ref, qt_out,
+    q_ref, modality, membership, xs, ds, merged, lsend, lrecv, msend, lmean, gsend, grecv,
     qpart, qr1, qs2, qr2, q3, qr3, q4, qf,
-    x_sem, d_sem, e_sem, m_sem, ls_sem, lr_sem, ms_sem, mr_sem, gs_sem, gr_sem,
+    in_sem, x_sem, d_sem, e_sem, m_sem, ls_sem, lr_sem, ms_sem, mr_sem, gs_sem, gr_sem,
     s1_sem, r1_sem, s2_sem, r2_sem, s3_sem, r3_sem, s4_sem, r4_sem,
     s5_sem, r5_sem,
 ):
@@ -123,12 +123,18 @@
     def rows_of(c, size):
         return pl.ds(pl.multiple_of(c * size, size), size)
 
+    twos = n_dp // 2
+    two_rows = 2 * step_rows
+
+    def two_of(s):
+        return (dp // 2 + 1 + s) % twos
+
     def err_copy(s):
-        at = rows_of((dp + 1 + s) % n_dp, step_rows)
+        at = rows_of(two_of(s), two_rows)
         return pltpu.make_async_copy(err_hbm.at[:, at, :], merged.at[:, at, :], e_sem.at[s])
 
     def merged_copy(s):
-        at = rows_of((dp + 1 + s) % n_dp, step_rows)
+        at = rows_of(two_of(s), two_rows)
         return pltpu.make_async_copy(merged.at[:, at, :], merged_hbm.at[:, at, :], m_sem.at[s])
 
     x_copies = [pltpu.make_async_copy(x_hbm.at[k], xs.at[k], x_sem.at[k]) for k in range(experts)]
@@ -136,7 +142,15 @@
     for k in range(experts):
         x_copies[k].start()
         d_copies[k].start()
-    for s in range(n_dp):
+    small = [
+        pltpu.make_async_copy(src, dst, in_sem.at[n])
+        for n, (src, dst) in enumerate(
+            ((q_hbm, q_ref), (modality_hbm, modality), (membership_hbm, membership))
+        )
+    ]
+    for copy in small:
+        copy.start()
+    for s in range(twos):
         err_copy(s).start()
 
     barrier = pltpu.get_barrier_semaphore()
@@ -149,6 +163,8 @@
     for k in range(experts):
         x_copies[k].wait()
         d_copies[k].wait()
+    for copy in small:
+        copy.wait()
 
     lane = lax.broadcasted_iota(jnp.int32, (1, width), 1)
 
@@ -156,13 +172,13 @@
         return remote(lsend.at[c], lrecv.at[src], ls_sem.at[c], lr_sem.at[src], c, ex)
 
     def left_step(s, carry):
-        c = (dp + 1 + s) % n_dp
-        at = rows_of(c, step_rows)
+        two = two_of(s)
+        at = rows_of(two, two_rows)
         err_copy(s).wait()
-        total = jnp.zeros((step_rows, width), F32)
+        total = jnp.zeros((two_rows, width), F32)
         for k in range(experts):
             xk = xs[k, :, at]
-            mine = jnp.zeros((step_rows, width), F32)
+            mine = jnp.zeros((two_rows, width), F32)
             for n in range(3):
                 cols = slice(n * (hidden // 3), (n + 1) * (hidden // 3))
                 grad = lax.dot_general(
@@ -173,19 +189,22 @@
                 mine += jnp.dot(both, q_ref[cols, :], preferred_element_type=F32)
             total += jnp.where(lane // rank == k, mine, 0.0)
         merged_copy(s).start()
-
-        @pl.when(s < n_dp - 1)
-        def _():
-            lsend[c] = total.astype(BF16)
-            left_copy(c, dp).start()
-
-        @pl.when(s == n_dp - 1)
-        def _():
-            lrecv[dp] = total.astype(BF16)
-
-        return carry
-
-    lax.fori_loop(0, n_dp, left_step, 0)
+        for h in range(2):
+            c = 2 * two + h
+            block = total[h * step_rows : (h + 1) * step_rows, :].astype(BF16)
+
+            @pl.when(c != dp)
+            def _():
+                lsend[c] = block
+                left_copy(c, dp).start()
+
+            @pl.when(c == dp)
+            def _():
+                lrecv[dp] = block
+
+        return carry
+
+    lax.fori_loop(0, twos, left_step, 0)
 
     def wait_left(s, carry):
         left_copy((dp + s) % n_dp, (dp + n_dp - s) % n_dp).wait_recv()
@@ -299,7 +318,6 @@
         p_t = lax.dot_general(inv_high, block, dims, preferred_element_type=F32)
         p_t += lax.dot_general(inv_low, block, dims, preferred_element_type=F32)
         pt_ref[:, j * step_rows : (j + 1) * step_rows] = p_t.astype(BF16)
-    pt_out[...] = pt_ref[...]
 
     def k_rows(k):
         return pl.ds(k * rank, rank)
@@ -447,10 +465,11 @@
     def drain_all(c, carry):
         for n in range(3):
             spread(c, n).wait_send()
-        merged_copy(c).wait()
         return carry
 
     lax.fori_loop(0, n_dp, drain_all, 0)
+    for s in range(twos):
+        merged_copy(s).wait()
     for k in range(experts):
         core_copy(k, 0).wait_send()
         core_copy(k, 1).wait_send()
@@ -459,11 +478,48 @@
         copy.wait_send()
 
 
-def residual_kernel(pt_ref, qt_ref, merged_ref, out_ref):
-    approx = lax.dot_general(
-        pt_ref[...], qt_ref[...], (((0,), (0,)), ((), ())), preferred_element_type=F32
-    )
-    out_ref[0] = (merged_ref[0].astype(F32) - approx).astype(BF16)
+def residual_kernel(
+    pt_ref, qt_ref, merged, err_hbm, q_hbm, stage, q_stage, m_sem, e_sem, q_sem
+):
+    experts, rows, hidden = merged.shape
+    rank = pt_ref.shape[0] // experts
+    pieces, size = stage.shape[:2]
+    per = rows // size
+
+    def place(ref, t):
+        return ref.at[t // per, pl.ds(pl.multiple_of((t % per) * size, size), size), :]
+
+    def load(t):
+        return pltpu.make_async_copy(place(merged, t), stage.at[t], m_sem.at[t])
+
+    def copy(t):
+        return pltpu.make_async_copy(stage.at[t], place(err_hbm, t), e_sem.at[t])
+
+    for t in range(pieces):
+        load(t).start()
+
+    def step(t, carry):
+        at = pl.ds(pl.multiple_of((t % per) * size, size), size)
+        of = pl.ds(pl.multiple_of((t // per) * rank, rank), rank)
+        approx = lax.dot_general(
+            pt_ref[of, at], qt_ref[of, :], (((0,), (0,)), ((), ())), preferred_element_type=F32
+        )
+        load(t).wait()
+        stage[t] = (stage[t].astype(F32) - approx).astype(BF16)
+        copy(t).start()
+        return carry
+
+    lax.fori_loop(0, pieces, step, 0)
+    q_stage[...] = qt_ref[...].T
+    q_copy = pltpu.make_async_copy(q_stage, q_hbm, q_sem)
+    q_copy.start()
+
+    def wait(t, carry):
+        copy(t).wait()
+        return carry
+
+    lax.fori_loop(0, pieces, wait, 0)
+    q_copy.wait()
 
 
 def tiled_form(n_dp, n_ex, x_act, d_out, error, q_init, modality, membership):
@@ -475,7 +531,6 @@
     group_size = membership.shape[0] // GROUPS
     any_spec = pl.BlockSpec(memory_space=pl.ANY)
     vmem = pl.BlockSpec(memory_space=pltpu.VMEM)
-    smem = pl.BlockSpec(memory_space=pltpu.SMEM)
     dma = pltpu.SemaphoreType.DMA
     merged, p_t, q_t = pl.pallas_call(
         functools.partial(compress_kernel, n_dp, n_ex, group_size),
@@ -484,9 +539,12 @@
             jax.ShapeDtypeStruct((width, rows), BF16),
             jax.ShapeDtypeStruct((width, hidden), BF16),
         ),
-        in_specs=[any_spec, any_spec, any_spec, vmem, smem, smem],
+        in_specs=[any_spec] * 6,
         out_specs=(any_spec, vmem, vmem),
         scratch_shapes=[
+            pltpu.VMEM((hidden, width), BF16),
+            pltpu.SMEM(modality.shape, jnp.int32),
+            pltpu.SMEM(membership.shape, jnp.int32),
             pltpu.VMEM((experts, tokens, rows), BF16),
             pltpu.VMEM((experts, tokens, hidden), BF16),
             pltpu.VMEM((experts, rows, hidden), BF16),
@@ -496,7 +554,6 @@
             pltpu.VMEM((n_dp, step_rows, width), BF16),
             pltpu.VMEM((experts // 2, rank, 2 * rank), F32),
             pltpu.VMEM((n_ex, experts // 2, rank, 2 * rank), F32),
-            pltpu.VMEM((width, rows), BF16),
             pltpu.VMEM((n_ex, width, slab), BF16),
             pltpu.VMEM((2, width, slab), BF16),
             pltpu.VMEM((width, slab), BF16),
@@ -505,7 +562,7 @@
             pltpu.VMEM((n_dp, part, slab), BF16),
             pltpu.VMEM((n_dp, part, slab), BF16),
             pltpu.VMEM((n_ex, width, slab), BF16),
-            dma((experts,)), dma((experts,)), dma((n_dp,)), dma((n_dp,)),
+            dma((3,)), dma((experts,)), dma((experts,)), dma((n_dp // 2,)), dma((n_dp // 2,)),
             dma((n_dp,)), dma((n_dp,)), dma((n_dp,)), dma((n_dp,)),
             dma((3,)), dma((3,)),
             dma((2, experts)), dma((2, experts)), dma((experts,)), dma((experts,)),
@@ -513,7 +570,7 @@
             dma((3, n_dp)), dma((3, n_dp)),
         ],
         compiler_params=pltpu.CompilerParams(
-            collective_id=0, has_side_effects=True, vmem_limit_bytes=50 * 2**20
+            collective_id=0, has_side_effects=True, vmem_limit_bytes=56 * 2**20
         ),
         cost_estimate=pl.CostEstimate(
             flops=12 * experts * rows * hidden * tokens // 4,
@@ -523,20 +580,25 @@
         name="compress",
     )(x_act[0], d_out[0], error[0], q_init, modality, membership)
     block = rows // 4
-    error_new = pl.pallas_call(
+    error_new, q_sum = pl.pallas_call(
         residual_kernel,
-        grid=(experts, rows // block),
-        out_shape=jax.ShapeDtypeStruct((experts, rows, hidden), BF16),
-        in_specs=[
-            pl.BlockSpec((rank, block), lambda k, r: (k, r)),
-            pl.BlockSpec((rank, hidden), lambda k, r: (k, 0)),
-            pl.BlockSpec((1, block, hidden), lambda k, r: (k, r, 0)),
+        out_shape=(
+            jax.ShapeDtypeStruct((experts, rows, hidden), BF16),
+            jax.ShapeDtypeStruct((hidden, width), BF16),
+        ),
+        in_specs=[vmem, vmem, any_spec],
+        out_specs=(any_spec, any_spec),
+        scratch_shapes=[
+            pltpu.VMEM((experts * rows // block, block, hidden), BF16),
+            pltpu.VMEM((hidden, width), BF16),
+            dma((experts * rows // block,)),
+            dma((experts * rows // block,)),
+            dma,
         ],
-        out_specs=pl.BlockSpec((1, block, hidden), lambda k, r: (k, r, 0)),
-        compiler_params=pltpu.CompilerParams(vmem_limit_bytes=32 * 2**20),
+        compiler_params=pltpu.CompilerParams(vmem_limit_bytes=56 * 2**20),
         name="residual",
     )(p_t, q_t, merged)
-    return (q_t.T[None], error_new[None])
+    return (q_sum[None], error_new[None])
 
 
 def tiles(n_dp, n_ex, x_act, d_out, error, q_init, modality, membership):

time: 95.7 us -> 87 us (0.909)
  local copies, waits for them, and re-layouts: 8.16 us -> 0 us
    unnamed x9 -> x0, local copies, waits for them, and re-layouts: 8.16 us -> none
    pallas_call x1, Pallas kernels: 76.1 us -> 74.4 us  [tiled_form(): pl.pallas_call(functools.partial(compress_kernel, n_dp, n_ex, group_size)...]
    pallas_call x1, Pallas kernels: 10.6 us -> 11.8 us  [tiled_form(): pl.pallas_call(residual_kernel, out_shape=(jax.ShapeDtypeStruct((experts,...]
where the time goes in v2:
time: 87 us; the launch traced here: 86.9 us
  Pallas kernels  86.2 us (99%)
    pallas_call x1, Pallas kernels, tiled_form(): pl.pallas_call(functools.partial(compress_kernel, n_dp, n_ex, group_size)...  74.4 us
    pallas_call x1, Pallas kernels, tiled_form(): pl.pallas_call(residual_kernel, out_shape=(jax.ShapeDtypeStruct((experts,...  11.8 us

profile of v2, /device:TPU:1, one launch (start us, length us, event | category | flops | bytes accessed | tf_op | source)
XLA Modules:
  0.0 86.9 jit_solution(2789474886291347983)
XLA Ops:
  0.6 74.4 %compress.1 = (bf16[4,1024,1536]{2,1,0:T(8,128)(2,1)}, bf16[256,1024]{1,0:T(8,128)(2,1)}, bf16[256,1536]{1,0:T(8,128)(2,1)}) custom-call(bf16[4,256,1024]{2,1,0:T(8,128)(2,1)} %bitcast.7, bf16[4,256,1536]{2,1,0:T(8,128)(2,1)} %bitcast.6, bf16[4,1024,1536]{2,1,0:T(8,128)(2,1)} %bitcast.5, bf16[1536,256]{1,0:T(8,128)(2,1)} %q_hbm.1, s32[4]{0:T(128)} %modality_hbm.1, ...), custom_call_target="tpu_custom_call" | custom-call | flops 4831838208 | bytes 25165824 | tf_op jit(solution)/shard_map/compress/pallas_call | solution.py:535
  75.1 11.8 %residual.1 = (bf16[4,1024,1536]{2,1,0:T(8,128)(2,1)}, bf16[1536,256]{1,0:T(8,128)(2,1)}) custom-call(bf16[256,1024]{1,0:T(8,128)(2,1)} %get-tuple-element.7.pt_ref, bf16[256,1536]{1,0:T(8,128)(2,1)} %get-tuple-element.8.qt_ref, bf16[4,1024,1536]{2,1,0:T(8,128)(2,1)} %get-tuple-element.9.merged), custom_call_target="tpu_custom_call" | custom-call | tf_op jit(solution)/shard_map/residual/pallas_call | solution.py:583

commit v3 on v2

--- a/solution.py
+++ b/solution.py
@@ -178,15 +178,13 @@
         total = jnp.zeros((two_rows, width), F32)
         for k in range(experts):
             xk = xs[k, :, at]
-            mine = jnp.zeros((two_rows, width), F32)
-            for n in range(3):
-                cols = slice(n * (hidden // 3), (n + 1) * (hidden // 3))
+            for n in range(hidden // 256):
+                cols = slice(n * 256, (n + 1) * 256)
                 grad = lax.dot_general(
                     xk, ds[k, :, cols], (((0,), (0,)), ((), ())), preferred_element_type=F32
                 )
-                both = (grad + merged[k, at, cols].astype(F32)).astype(BF16)
-                merged[k, at, cols] = both
-                mine += jnp.dot(both, q_ref[cols, :], preferred_element_type=F32)
+                merged[k, at, cols] = (grad + merged[k, at, cols].astype(F32)).astype(BF16)
+            mine = jnp.dot(merged[k, at, :], q_ref[...], preferred_element_type=F32)
             total += jnp.where(lane // rank == k, mine, 0.0)
         merged_copy(s).start()
         for h in range(2):
@@ -283,17 +281,25 @@
         here = low if odd == 0 else jnp.logical_not(low)
         work.append(jnp.where(here, a, jnp.where(unit, 1.0, 0.0)))
     done = [[], []]
-    for j in range(rank):
-        r = j % 8
-        left_rows = rank - (j - r)
-        below = lax.broadcasted_iota(jnp.int32, (1, left_rows, 1), 1) > r
+    panel = 4
+    for j in range(0, rank, panel):
+        left_rows = rank - j // 8 * 8
+        at_row = lax.broadcasted_iota(jnp.int32, (1, left_rows, 1), 1)
         for odd in range(2):
             w = work[odd]
-            at = j + odd * rank
-            pivot = w[:, r : r + 1, :]
-            scaled = pivot / w[:, r : r + 1, at : at + 1]
-            work[odd] = w - jnp.where(below, w[:, :, at : at + 1], 0.0) * scaled
-        if r == 7:
+            columns = [
+                jnp.broadcast_to(w[:, :, at : at + 1], w.shape)
+                for at in range(j + odd * rank, j + odd * rank + panel)
+            ]
+            for m in range(panel):
+                r = j % 8 + m
+                inverse_pivot = 1.0 / columns[m][:, r : r + 1, :]
+                factor = jnp.where(at_row > r, columns[m], 0.0) * inverse_pivot
+                for n in range(m + 1, panel):
+                    columns[n] = columns[n] - factor * columns[n][:, r : r + 1, :]
+                w = w - factor * w[:, r : r + 1, :]
+            work[odd] = w
+        if (j + panel) % 8 == 0:
             for odd in range(2):
                 done[odd].append(work[odd][:, :8, :])
                 work[odd] = work[odd][:, 8:, :]
@@ -501,11 +507,14 @@
     def step(t, carry):
         at = pl.ds(pl.multiple_of((t % per) * size, size), size)
         of = pl.ds(pl.multiple_of((t // per) * rank, rank), rank)
-        approx = lax.dot_general(
-            pt_ref[of, at], qt_ref[of, :], (((0,), (0,)), ((), ())), preferred_element_type=F32
-        )
+        p_rows = pt_ref[of, at]
         load(t).wait()
-        stage[t] = (stage[t].astype(F32) - approx).astype(BF16)
+        for n in range(hidden // 256):
+            cols = slice(n * 256, (n + 1) * 256)
+            approx = lax.dot_general(
+                p_rows, qt_ref[of, cols], (((0,), (0,)), ((), ())), preferred_element_type=F32
+            )
+            stage[t, :, cols] = (stage[t, :, cols].astype(F32) - approx).astype(BF16)
         copy(t).start()
         return carry
 
@@ -609,12 +618,11 @@
         n_ex == 4
         and experts % 2 == 0
         and 2 * rank == 128
-        and experts % 2 == 0
         and rank % (width // n_dp) == 0
         and (width // n_dp) % 16 == 0
         and (rows // n_dp) % 128 == 0
         and (hidden // n_ex) % 128 == 0
-        and (hidden // 3) % 128 == 0
+        and hidden % 256 == 0
     )
 
 

time: 87 us -> 83.6 us (0.961)
  Pallas kernels: 86.2 us -> 82.8 us
    pallas_call x1, Pallas kernels: 74.4 us -> 71.8 us  [tiled_form(): pl.pallas_call(functools.partial(compress_kernel, n_dp, n_ex, group_size)...]
    pallas_call x1, Pallas kernels: 11.8 us -> 10.9 us  [tiled_form(): pl.pallas_call(residual_kernel, out_shape=(jax.ShapeDtypeStruct((experts,...]
where the time goes in v3:
time: 83.6 us; the launch traced here: 83.4 us
  Pallas kernels  82.8 us (99%)
    pallas_call x1, Pallas kernels, tiled_form(): pl.pallas_call(functools.partial(compress_kernel, n_dp, n_ex, group_size)...  71.8 us
    pallas_call x1, Pallas kernels, tiled_form(): pl.pallas_call(residual_kernel, out_shape=(jax.ShapeDtypeStruct((experts,...  10.9 us

profile of v3, /device:TPU:1, one launch (start us, length us, event | category | flops | bytes accessed | tf_op | source)
XLA Modules:
  0.0 83.4 jit_solution(11435140544773918004)
XLA Ops:
  0.6 71.8 %compress.1 = (bf16[4,1024,1536]{2,1,0:T(8,128)(2,1)}, bf16[256,1024]{1,0:T(8,128)(2,1)}, bf16[256,1536]{1,0:T(8,128)(2,1)}) custom-call(bf16[4,256,1024]{2,1,0:T(8,128)(2,1)} %bitcast.7, bf16[4,256,1536]{2,1,0:T(8,128)(2,1)} %bitcast.6, bf16[4,1024,1536]{2,1,0:T(8,128)(2,1)} %bitcast.5, bf16[1536,256]{1,0:T(8,128)(2,1)} %q_hbm.1, s32[4]{0:T(128)} %modality_hbm.1, ...), custom_call_target="tpu_custom_call" | custom-call | flops 4831838208 | bytes 25165824 | tf_op jit(solution)/shard_map/compress/pallas_call | solution.py:544
  72.5 10.9 %residual.1 = (bf16[4,1024,1536]{2,1,0:T(8,128)(2,1)}, bf16[1536,256]{1,0:T(8,128)(2,1)}) custom-call(bf16[256,1024]{1,0:T(8,128)(2,1)} %get-tuple-element.7.pt_ref, bf16[256,1536]{1,0:T(8,128)(2,1)} %get-tuple-element.8.qt_ref, bf16[4,1024,1536]{2,1,0:T(8,128)(2,1)} %get-tuple-element.9.merged), custom_call_target="tpu_custom_call" | custom-call | tf_op jit(solution)/shard_map/residual/pallas_call | solution.py:592
